TPU v7x, 32 devices: a whole 2x2x4 slice. The times are simulated.
32 devices in a mesh: section: 2 (over x), dp: 16 (over z, y, core).
Axes of the slice: x: 2, y: 2, z: 4, core: 2. Of those that a mesh axis runs over, the one named last changes fastest.
Arguments:
- tokens: bfloat16 [16384, 768], P('dp'), may hold values from -6 to 6
- segment_ids: int32 [16384], P('dp'), may hold values from 0 to 511, as said below
- cotangent: bfloat16 [16384, 768], P('dp'), may hold values from -6 to 6
- norm_gains: float32 [2, 2, 768], P('section'), may hold values from 0.5 to 1.5
- mixing_table: bfloat16 [2, 12, 512, 512], P('section'), may hold values from -8 to 8
- value_weight: bfloat16 [2, 768, 768], P('section'), may hold values from -0.21875 to 0.21875
- out_weight: bfloat16 [2, 768, 768], P('section'), may hold values from -0.625 to 0.625
- up_weight: bfloat16 [2, 768, 3072], P('section'), may hold values from -0.21875 to 0.21875
- down_weight: bfloat16 [2, 3072, 768], P('section'), may hold values from -0.109375 to 0.109375
Outputs:
- layer_outputs: bfloat16 [2, 16384, 768], P('section', 'dp')
- stream_grads: float32 [2, 16384, 768], P('section', 'dp')
- gains_grad: float32 [2, 2, 768], P('section', None, 'dp')
- mixing_grad: float32 [2, 12, 512, 512], P('section', None, 'dp')
- value_grad: float32 [2, 768, 768], P('section', None, 'dp')
- out_grad: float32 [2, 768, 768], P('section', None, 'dp')
- up_grad: float32 [2, 768, 3072], P('section', None, 'dp')
- down_grad: float32 [2, 3072, 768], P('section', None, 'dp')
Inputs may be any that keep to these rules, and one draw needn't show every extreme that they name: `segment_ids`: within each aligned row of 512 tokens, the id of a token is the position in its row of the first token of its document, so ids never fall within a row and start at 0; the last token of every row is a document of its own.
All inputs are finite; a program needn't handle non-finite values.
Results may differ from a plain program's by a relative error of at most 0.013.
Values may be sent and summed in bfloat16 or wider, within the bound.
No kernel may reach another device: no remote copies, remote signals or barrier semaphores. Data moves between devices by JAX's collectives and lax.ppermute only.
A program may use at most 256 MiB of HBM per device.

v0:
```python
import jax
import jax.numpy as jnp
from jax import lax
from jax.sharding import PartitionSpec as P

L = 512
MICRO = 2


eps_norm = 1e-06


def from_behind(shard, axis, by):
    devices = lax.axis_size(axis)
    pairs = [(i, i + by) for i in range(devices) if 0 <= i + by < devices]
    return lax.ppermute(shard, axis, pairs)


def rms_scale(values):
    return lax.rsqrt(jnp.mean(values * values, axis=-1, keepdims=True) + eps_norm)


def mixing_probs(mix_table, seg_rows, causal):
    length = seg_rows.shape[1]
    same_doc = seg_rows[:, :, None] == seg_rows[:, None, :]
    row_pos = lax.broadcasted_iota(jnp.int32, (length, length), 0)
    col_pos = lax.broadcasted_iota(jnp.int32, (length, length), 1)
    allowed = same_doc & jnp.logical_or(col_pos <= row_pos, jnp.logical_not(causal))[None]
    scores = jnp.where(allowed[:, None], mix_table[None], -1e30)
    peak = jnp.max(scores, axis=-1, keepdims=True)
    expo = jnp.exp(scores - peak)
    return expo / jnp.sum(expo, axis=-1, keepdims=True)


def layer_forward(layer_in, seg_rows, weights, causal):
    gain_pair, mix_table, w_value, w_out, w_up, w_down = weights
    seqs, length = seg_rows.shape
    heads = mix_table.shape[0]
    width = layer_in.shape[1]
    scale_one = rms_scale(layer_in)
    normed_one = (layer_in * scale_one * gain_pair[0]).astype(jnp.bfloat16)
    values_low = jnp.dot(normed_one, w_value, preferred_element_type=jnp.float32).astype(
        jnp.bfloat16
    )
    prob_full = mixing_probs(mix_table, seg_rows, causal)
    prob_low = prob_full.astype(jnp.bfloat16)
    per_head = values_low.reshape(seqs, length, heads, width // heads)
    mixed = jnp.einsum("shij,sjhd->sihd", prob_low, per_head, preferred_element_type=jnp.float32)
    mixed_low = mixed.reshape(layer_in.shape).astype(jnp.bfloat16)
    residual_mid = layer_in + jnp.dot(mixed_low, w_out, preferred_element_type=jnp.float32)
    scale_two = rms_scale(residual_mid)
    normed_two = (residual_mid * scale_two * gain_pair[1]).astype(jnp.bfloat16)
    pre_act = jnp.dot(normed_two, w_up, preferred_element_type=jnp.float32)
    act_low = jax.nn.gelu(pre_act).astype(jnp.bfloat16)
    result = residual_mid + jnp.dot(act_low, w_down, preferred_element_type=jnp.float32)
    return (
        result,
        (
            scale_one,
            normed_one,
            values_low,
            prob_full,
            prob_low,
            mixed_low,
            residual_mid,
            scale_two,
            normed_two,
            pre_act,
            act_low,
        ),
    )


def norm_backward(grad_norm, values, scale, gain):
    normed_hat = values * scale
    gain_grad = jnp.sum(grad_norm * normed_hat, axis=0)
    scaled = grad_norm * gain
    grad_values = scale * (
        scaled - normed_hat * jnp.mean(scaled * normed_hat, axis=-1, keepdims=True)
    )
    return (grad_values, gain_grad)


def layer_backward(grad_out, layer_in, saved_parts, weights):
    gain_pair, mix_table, w_value, w_out, w_up, w_down = weights
    (
        scale_one,
        normed_one,
        values_low,
        prob_full,
        prob_low,
        mixed_low,
        residual_mid,
        scale_two,
        normed_two,
        pre_act,
        act_low,
    ) = saved_parts
    seqs, heads, length = (prob_full.shape[0], prob_full.shape[1], prob_full.shape[2])
    width = layer_in.shape[1]
    grad_low = grad_out.astype(jnp.bfloat16)
    down_g = jnp.einsum("tf,td->fd", act_low, grad_low, preferred_element_type=jnp.float32)
    grad_act = jnp.einsum("td,fd->tf", grad_low, w_down, preferred_element_type=jnp.float32)
    unused, gelu_back = jax.vjp(jax.nn.gelu, pre_act)
    grad_pre = gelu_back(grad_act)[0].astype(jnp.bfloat16)
    up_g = jnp.einsum("td,tf->df", normed_two, grad_pre, preferred_element_type=jnp.float32)
    grad_norm_two = jnp.einsum("tf,df->td", grad_pre, w_up, preferred_element_type=jnp.float32)
    grad_mid_norm, gain_two_g = norm_backward(grad_norm_two, residual_mid, scale_two, gain_pair[1])
    grad_mid = grad_out + grad_mid_norm
    grad_mid_low = grad_mid.astype(jnp.bfloat16)
    out_g = jnp.einsum("te,td->ed", mixed_low, grad_mid_low, preferred_element_type=jnp.float32)
    grad_mixed = jnp.einsum("td,ed->te", grad_mid_low, w_out, preferred_element_type=jnp.float32)
    grad_mixed_low = grad_mixed.astype(jnp.bfloat16).reshape(seqs, length, heads, width // heads)
    per_head = values_low.reshape(seqs, length, heads, width // heads)
    grad_prob = jnp.einsum(
        "sihd,sjhd->shij", grad_mixed_low, per_head, preferred_element_type=jnp.float32
    )
    grad_values = jnp.einsum(
        "shij,sihd->sjhd", prob_low, grad_mixed_low, preferred_element_type=jnp.float32
    )
    grad_values_low = grad_values.reshape(layer_in.shape).astype(jnp.bfloat16)
    grad_scores = prob_full * (grad_prob - jnp.sum(grad_prob * prob_full, axis=-1, keepdims=True))
    table_g = jnp.sum(grad_scores, axis=0)
    value_g = jnp.einsum(
        "td,te->de", normed_one, grad_values_low, preferred_element_type=jnp.float32
    )
    grad_norm_one = jnp.einsum(
        "te,de->td", grad_values_low, w_value, preferred_element_type=jnp.float32
    )
    grad_in_norm, gain_one_g = norm_backward(grad_norm_one, layer_in, scale_one, gain_pair[0])
    grad_in = grad_mid + grad_in_norm
    return (grad_in, (jnp.stack([gain_one_g, gain_two_g]), table_g, value_g, out_g, up_g, down_g))


def add_grads(totals, extra):
    if totals is None:
        return extra
    return tuple((left + right for left, right in zip(totals, extra)))


def shards(
    tokens,
    segment_ids,
    cotangent,
    norm_gains,
    mixing_table,
    value_weight,
    out_weight,
    up_weight,
    down_weight,
):
    section_index = lax.axis_index("section")
    is_first = section_index == 0
    causal = section_index == 1
    micro_count = MICRO
    block_rows = tokens.shape[0] // micro_count
    seqs = block_rows // L
    width = tokens.shape[1]
    weights = (
        norm_gains[0],
        mixing_table[0].astype(jnp.float32),
        value_weight[0],
        out_weight[0],
        up_weight[0],
        down_weight[0],
    )
    received = jnp.zeros((block_rows, width), jnp.bfloat16)
    inputs = jnp.zeros((micro_count, block_rows, width), jnp.float32)
    outputs = jnp.zeros((micro_count, block_rows, width), jnp.float32)
    for tick_step in range(micro_count + 1):
        mb_index = jnp.where(is_first, min(tick_step, micro_count - 1), max(tick_step - 1, 0))
        is_valid = jnp.where(is_first, tick_step < micro_count, tick_step >= 1)
        own_rows = lax.dynamic_slice_in_dim(tokens, mb_index * block_rows, block_rows, 0).astype(
            jnp.float32
        )
        layer_in = jnp.where(is_first, own_rows, received.astype(jnp.float32))
        seg_rows = lax.dynamic_slice_in_dim(
            segment_ids, mb_index * block_rows, block_rows, 0
        ).reshape(seqs, L)
        result, saved_parts = layer_forward(layer_in, seg_rows, weights, causal)
        inputs = inputs.at[mb_index].set(jnp.where(is_valid, layer_in, inputs[mb_index]))
        outputs = outputs.at[mb_index].set(jnp.where(is_valid, result, outputs[mb_index]))
        if tick_step < micro_count:
            received = from_behind(result.astype(jnp.bfloat16), "section", 1)
    returned = jnp.zeros((block_rows, width), jnp.bfloat16)
    stream_grad = jnp.zeros((micro_count, block_rows, width), jnp.float32)
    totals = None
    for tick_step in range(micro_count + 1):
        mb_index = jnp.where(
            is_first,
            min(micro_count - tick_step, micro_count - 1),
            max(micro_count - 1 - tick_step, 0),
        )
        is_valid = jnp.where(is_first, tick_step >= 1, tick_step < micro_count)
        cot_rows = lax.dynamic_slice_in_dim(cotangent, mb_index * block_rows, block_rows, 0).astype(
            jnp.float32
        )
        upstream = jnp.where(is_first, returned.astype(jnp.float32), cot_rows)
        layer_in = inputs[mb_index]
        seg_rows = lax.dynamic_slice_in_dim(
            segment_ids, mb_index * block_rows, block_rows, 0
        ).reshape(seqs, L)
        unused, saved_parts = layer_forward(layer_in, seg_rows, weights, causal)
        grad_in, grads = layer_backward(upstream, layer_in, saved_parts, weights)
        stream_grad = stream_grad.at[mb_index].set(
            jnp.where(is_valid, grad_in, stream_grad[mb_index])
        )
        masked = tuple((jnp.where(is_valid, piece, jnp.zeros_like(piece)) for piece in grads))
        totals = add_grads(totals, masked)
        if tick_step < micro_count:
            returned = from_behind(grad_in.astype(jnp.bfloat16), "section", -1)
    totals = (
        lax.psum_scatter(totals[0], "dp", scatter_dimension=1, tiled=True),
        lax.psum_scatter(totals[1], "dp", scatter_dimension=1, tiled=True),
        lax.psum_scatter(totals[2], "dp", scatter_dimension=1, tiled=True),
        lax.psum_scatter(totals[3], "dp", scatter_dimension=1, tiled=True),
        lax.psum_scatter(totals[4], "dp", scatter_dimension=1, tiled=True),
        lax.psum_scatter(totals[5], "dp", scatter_dimension=1, tiled=True),
    )
    both_out = outputs.reshape(micro_count * block_rows, width).astype(jnp.bfloat16)[None]
    both_grads = stream_grad.reshape(micro_count * block_rows, width)[None]
    return (
        both_out,
        both_grads,
        totals[0][None],
        totals[1][None],
        totals[2][None],
        totals[3][None],
        totals[4][None],
        totals[5][None],
    )


def solution(mesh):
    placed = (
        P("dp", None),
        P("dp"),
        P("dp", None),
        P("section", None, None),
        P("section", None, None, None),
        P("section", None, None),
        P("section", None, None),
        P("section", None, None),
        P("section", None, None),
    )
    return jax.shard_map(
        shards,
        mesh=mesh,
        in_specs=placed,
        out_specs=(
            P("section", "dp", None),
            P("section", "dp", None),
            P("section", None, "dp"),
            P("section", None, "dp", None),
            P("section", None, "dp"),
            P("section", None, "dp"),
            P("section", None, "dp"),
            P("section", None, "dp"),
        ),
        check_vma=False,
    )
```

profile of v0, /device:TPU:0, one launch (start us, length us, event | category | flops | bytes accessed | tf_op | source)
XLA Modules:
  0.0 921.7 jit_solution(11208433445673700401)
XLA Ops:
  12.7 8.7 copy.64
  22.2 6.0 fusion.11
  28.3 7.3 fusion.14
  35.8 10.6 %fusion.85 = (bf16[12,512,512]{1,2,0:T(8,128)(2,1)}, bf16[12,512,512]{1,2,0:T(8,128)(2,1)S(1)}, bf16[12,512,512]{1,2,0:T(8,128)(2,1)}) fusion(bf16[1,12,512,512]{2,3,1,0:T(8,128)(2,1)S(1)} %copy-done.9, f32[12,512]{1,0:T(8,128)S(1)} %get-tuple-element.140, f32[12,512]{1,0:T(8,128)S(1)} %get-tuple-element.143, pred[512,512]{0,1:T(8,128)(4,1)S(1)} %get-tuple-element.196, ...), kind=kLoop, calls=%fused_computation.102 | loop fusion | flops 40894464 | bytes 26099712 | tf_op jit(solution)/shard_map/reshape.284
  65.4 14.6 %collective-permute-done = bf16[512,768]{1,0:T(8,128)(2,1)S(1)} collective-permute-done((bf16[512,768]{1,0:T(8,128)(2,1)S(1)}, bf16[512,768]{1,0:T(8,128)(2,1)S(1)}, u32[]{:S(2)}, u32[]{:S(2)}) %collective-permute-start) | collective-permute-done | bytes 786464 | tf_op jit(solution)/shard_map/ppermute | solution.py:16
  95.4 5.5 fusion.154
  100.8 5.8 collective-permute-start.1
  109.4 12.1 %collective-permute-done.1 = bf16[512,768]{1,0:T(8,128)(2,1)} collective-permute-done((bf16[512,768]{1,0:T(8,128)(2,1)}, bf16[512,768]{1,0:T(8,128)(2,1)}, u32[]{:S(2)}, u32[]{:S(2)}) %collective-permute-start.1) | collective-permute-done | bytes 786464 | tf_op jit(solution)/shard_map/ppermute | solution.py:16
  150.8 6.1 fusion.44
  166.1 5.2 convolution_convert_fusion.13
  178.9 15.4 %collective-permute-done.2 = bf16[512,768]{1,0:T(8,128)(2,1)S(1)} collective-permute-done((bf16[512,768]{1,0:T(8,128)(2,1)S(1)}, bf16[512,768]{1,0:T(8,128)(2,1)S(1)}, u32[]{:S(2)}, u32[]{:S(2)}) %collective-permute-start.2) | collective-permute-done | bytes 786464 | tf_op jit(solution)/shard_map/ppermute | solution.py:16
  194.4 6.6 fusion.51
  207.2 6.0 convolution_convert_fusion.11
  213.2 13.0 %fusion.1 = f32[12,512,512]{1,2,0:T(8,128)} fusion(bf16[512,12,64]{0,2,1:T(8,128)(2,1)} %bitcast.398, bf16[512,12,64]{0,2,1:T(8,128)(2,1)S(1)} %bitcast.392, bf16[1,12,512,512]{2,3,1,0:T(8,128)(2,1)} %copy.64, f32[12,512]{1,0:T(8,128)} %copy-done.81, f32[12,512]{1,0:T(8,128)} %copy-done.78, pred[512,512]{0,1:T(8,128)(4,1)} %copy-done.67), kind=kOutput, calls=%fused_computation.1 | convolution fusion | flops 418388480 | bytes 20758528 | tf_op jit(solution)/shard_map/sub | solution.py:122
  226.2 7.7 fusion.268
  252.4 13.5 %collective-permute-done.3 = bf16[512,768]{1,0:T(8,128)(2,1)S(1)} collective-permute-done((bf16[512,768]{1,0:T(8,128)(2,1)S(1)}, bf16[512,768]{1,0:T(8,128)(2,1)S(1)}, u32[]{:S(2)}, u32[]{:S(2)}) %collective-permute-start.3) | collective-permute-done | bytes 786464 | tf_op jit(solution)/shard_map/ppermute | solution.py:16
  265.9 5.9 fusion.58
  279.9 5.9 convolution_convert_fusion.9
  285.8 13.1 %fusion = f32[12,512,512]{1,2,0:T(8,128)} fusion(bf16[512,12,64]{0,2,1:T(8,128)(2,1)} %bitcast.401, bf16[512,12,64]{0,2,1:T(8,128)(2,1)S(1)} %bitcast.395, bf16[1,12,512,512]{2,3,1,0:T(8,128)(2,1)} %copy.64, f32[12,512]{1,0:T(8,128)} %copy-done.82, f32[12,512]{1,0:T(8,128)} %copy-done.79, pred[512,512]{0,1:T(8,128)(4,1)} %copy-done.68), kind=kOutput, calls=%fused_computation | convolution fusion | flops 418388480 | bytes 20758528 | tf_op jit(solution)/shard_map/sub | solution.py:122
  298.9 7.7 fusion.269
  312.2 29.5 %select_add_fusion = f32[12,512,512]{1,2,0:T(8,128)} fusion(f32[12,512,512]{1,2,0:T(8,128)} %fusion.269, f32[12,512,512]{1,2,0:T(8,128)} %fusion, f32[12,512,512]{1,2,0:T(8,128)} %fusion.268, f32[12,512,512]{1,2,0:T(8,128)} %fusion.1, pred[]{:T(512)S(6)} %eq.40, pred[]{:T(512)S(6)} %select_n.242, f32[12,512]{1,0:T(8,128)} %copy-done.80, ...), kind=kOutput, calls=%fused_computation.37 | convolution fusion | flops 883956224 | bytes 71712768 | tf_op jit(solution)/shard_map/sub | solution.py:122
  341.7 18.4 %copy.82 = f32[12,512,512]{2,0,1:T(8,128)} copy(f32[12,512,512]{1,2,0:T(8,128)} %select_add_fusion) | data formatting | bytes 25165824 | tf_op jit(solution)/shard_map/add | solution.py:138
  379.8 6.4 fusion.258
  386.2 14.4 %select_add_fusion.2 = f32[768,3072]{0,1:T(8,128)} fusion(f32[768,3072]{0,1:T(8,128)} %fusion.258, f32[768,3072]{0,1:T(8,128)S(1)} %fusion.257, bf16[512,3072]{1,0:T(8,128)(2,1)} %copy-done.53, pred[]{:T(512)S(6)} %eq.40, pred[]{:T(512)S(6)} %select_n.242, f32[512,768]{1,0:T(8,128)S(1)} %copy-done.14, f32[512]{0:T(512)S(1)} %add_rsqrt_fusion, ...), kind=kOutput, calls=%fused_computation.48 | convolution fusion | flops 2426535936 | bytes 33035266 | tf_op jit(solution)/shard_map/td,tf->df/dot_general | solution.py:106
  400.9 5.5 fusion.123
  406.5 10.2 %fusion.124 = f32[3072,768]{0,1:T(8,128)} fusion(f32[512,3072]{1,0:T(8,128)} %copy-done.49, bf16[512,768]{1,0:T(8,128)(2,1)S(1)} %copy-done.72, pred[]{:T(512)S(6)} %eq.40, bf16[1024,768]{1,0:T(8,128)(2,1)S(1)} %copy-done.47, s32[]{:T(128)S(6)} %select_n.239), kind=kOutput, calls=%fused_computation.137 | convolution fusion | flops 2431647744 | bytes 17301508 | tf_op jit(solution)/shard_map/tf,td->fd/dot_general | solution.py:102
  416.7 9.4 %select_add_fusion.1 = f32[3072,768]{0,1:T(8,128)} fusion(f32[3072,768]{0,1:T(8,128)} %fusion.124, f32[3072,768]{0,1:T(8,128)S(1)} %fusion.123, pred[]{:T(512)S(6)} %eq.40, pred[]{:T(512)S(6)} %select_n.242, f32[512,3072]{1,0:T(8,128)S(1)} %bitcast.372, bf16[512,768]{1,0:T(8,128)(2,1)S(1)} %copy-done.52, bf16[1024,768]{1,0:T(8,128)(2,1)} %param.29), kind=kOutput, calls=%fused_computation.47 | convolution fusion | flops 2441084928 | bytes 36177408 | tf_op jit(solution)/shard_map/tf,td->fd/dot_general | solution.py:102
  458.3 92.2 %reduce-scatter.9.cloned.1.call-done = f32[12,32,512]{2,0,1:T(8,128)} async-done(((f32[12,512,512]{2,0,1:T(8,128)}), f32[12,32,512]{2,0,1:T(8,128)}) %reduce-scatter.9.cloned.1.call-update) | async-done | bytes 786448 | tf_op jit(solution)/shard_map/reduce_scatter | solution.py:214
  553.1 64.2 %reduce-scatter.13.cloned.1.call-done = f32[768,48]{0,1:T(8,128)} async-done(((f32[768,768]{0,1:T(8,128)}), f32[768,48]{0,1:T(8,128)}) %reduce-scatter.13.cloned.1.call-update) | async-done | bytes 147472 | tf_op jit(solution)/shard_map/reduce_scatter | solution.py:216
  617.2 66.2 %reduce-scatter.11.cloned.1.call-done = f32[768,48]{0,1:T(8,128)} async-done(((f32[768,768]{0,1:T(8,128)}), f32[768,48]{0,1:T(8,128)}) %reduce-scatter.11.cloned.1.call-update) | async-done | bytes 147472 | tf_op jit(solution)/shard_map/reduce_scatter | solution.py:215
  683.5 115.5 %reduce-scatter.15.cloned.1.call-done = f32[768,192]{0,1:T(8,128)} async-done(((f32[768,3072]{0,1:T(8,128)}), f32[768,192]{0,1:T(8,128)}) %reduce-scatter.15.cloned.1.call-update) | async-done | bytes 589840 | tf_op jit(solution)/shard_map/reduce_scatter | solution.py:217
  798.9 115.7 %reduce-scatter.17.cloned.1.call-done = f32[3072,48]{0,1:T(8,128)} async-done(((f32[3072,768]{0,1:T(8,128)}), f32[3072,48]{0,1:T(8,128)}) %reduce-scatter.17.cloned.1.call-update) | async-done | bytes 589840 | tf_op jit(solution)/shard_map/reduce_scatter | solution.py:218
  (380 shorter events, 181.2 us)
Async XLA Ops:
  7.2 449.7 %reduce-scatter.19.cloned.1.call-start = ((), (), s32[]{:S(2)}) async-start(), calls=%async_computation.11 | async-start | bytes 417792
  21.7 14.0 %copy-start.68 = (pred[512,512]{0,1:T(8,128)(4,1)}, pred[512,512]{0,1:T(8,128)(4,1)S(1)}, u32[]{:S(2)}) copy-start(pred[512,512]{0,1:T(8,128)(4,1)S(1)} %fusion.197) | copy-start | bytes 786436
  22.2 13.5 %copy-start.66 = (pred[512,512]{0,1:T(8,128)(4,1)}, pred[512,512]{0,1:T(8,128)(4,1)S(1)}, u32[]{:S(2)}) copy-start(pred[512,512]{0,1:T(8,128)(4,1)S(1)} %get-tuple-element.196) | copy-start | bytes 786436
  28.3 22.9 %slice-start.4 = ((s8[4718592]{0:T(1024)(128)(4,1)}), s8[4194304]{0:T(1024)(128)(4,1)S(1)}, s32[]{:S(2)}) async-start(s8[4718592]{0:T(1024)(128)(4,1)} %bitcast.373), calls=%async_computation.16 | async-start | bytes 8388608
  35.7 15.5 %slice-start.5 = ((s8[4718592]{0:T(1024)(128)(4,1)}), s8[524288]{0:T(1024)(128)(4,1)S(1)}, s32[]{:S(2)}) async-start(s8[4718592]{0:T(1024)(128)(4,1)} %bitcast.373), calls=%async_computation.17 | async-start | bytes 1048576
  58.4 21.6 %collective-permute-start = (bf16[512,768]{1,0:T(8,128)(2,1)S(1)}, bf16[512,768]{1,0:T(8,128)(2,1)S(1)}, u32[]{:S(2)}, u32[]{:S(2)}) collective-permute-start(bf16[512,768]{1,0:T(8,128)(2,1)S(1)} %fusion.163), channel_id=1, source_target_pairs={{0,16},{1,17},{2,18},{3,19},{4,20},{5,21},{6,22},{7,23},{8,24},{9,... | collective-permute-start | bytes 2359304 | tf_op jit(solution)/shard_map/ppermute | solution.py:16
  100.8 20.7 %collective-permute-start.1 = (bf16[512,768]{1,0:T(8,128)(2,1)}, bf16[512,768]{1,0:T(8,128)(2,1)}, u32[]{:S(2)}, u32[]{:S(2)}) collective-permute-start(bf16[512,768]{1,0:T(8,128)(2,1)} %get-tuple-element.181), channel_id=1, source_target_pairs={{0,16},{1,17},{2,18},{3,19},{4,20},{5,21},{6,22},{7,23},{8,24},{9,... | collective-permute-start | bytes 2359304 | tf_op jit(solution)/shard_map/ppermute | solution.py:16
  123.8 49.3 %copy-start.11 = (f32[512,768]{1,0:T(8,128)}, f32[512,768]{1,0:T(8,128)S(1)}, u32[]{:S(2)}) copy-start(f32[512,768]{1,0:T(8,128)S(1)} %get-tuple-element.166) | copy-start | bytes 4718596
  123.9 49.1 %copy-start.83 = (f32[512]{0:T(512)}, f32[512]{0:T(512)S(1)}, u32[]{:S(2)}) copy-start(f32[512]{0:T(512)S(1)} %add_rsqrt_fusion.5) | copy-start | bytes 6148
  125.6 119.8 %copy-start.84 = (f32[512]{0:T(512)}, f32[512]{0:T(512)S(1)}, u32[]{:S(2)}) copy-start(f32[512]{0:T(512)S(1)} %add_rsqrt_fusion.3) | copy-start | bytes 6148
  144.0 16.3 %copy-start.15 = (f32[512,768]{1,0:T(8,128)}, f32[512,768]{1,0:T(8,128)S(1)}, u32[]{:S(2)}) copy-start(f32[512,768]{1,0:T(8,128)S(1)} %get-tuple-element.185) | copy-start | bytes 4718596
  144.1 16.3 %copy-start.73 = (f32[512]{0:T(512)}, f32[512]{0:T(512)S(1)}, u32[]{:S(2)}) copy-start(f32[512]{0:T(512)S(1)} %add_rsqrt_fusion.4) | copy-start | bytes 6148
  173.1 21.3 %slice-start.22 = ((s8[4718592]{0:T(1024)(128)(4,1)}), s8[4194304]{0:T(1024)(128)(4,1)S(1)}, s32[]{:S(2)}) async-start(s8[4718592]{0:T(1024)(128)(4,1)} %bitcast.429), calls=%async_computation.34 | async-start | bytes 8388608
  174.7 19.6 %collective-permute-start.2 = (bf16[512,768]{1,0:T(8,128)(2,1)S(1)}, bf16[512,768]{1,0:T(8,128)(2,1)S(1)}, u32[]{:S(2)}, u32[]{:S(2)}) collective-permute-start(bf16[512,768]{1,0:T(8,128)(2,1)S(1)} %get-tuple-element.163), channel_id=1, source_target_pairs={{16,0},{17,1},{18,2},{19,3},{20,4},{21,5},{22,6},{23,7},{24,8},{25... | collective-permute-start | bytes 2359304 | tf_op jit(solution)/shard_map/ppermute | solution.py:16
  176.2 27.7 %copy-start.75 = (f32[512]{0:T(512)}, f32[512]{0:T(512)S(1)}, u32[]{:S(2)}) copy-start(f32[512]{0:T(512)S(1)} %add_rsqrt_fusion.2) | copy-start | bytes 6148
  176.2 18.1 %copy-start.45 = (bf16[1024,768]{1,0:T(8,128)(2,1)S(1)}, bf16[1024,768]{1,0:T(8,128)(2,1)}, u32[]{:S(2)}) copy-start(bf16[1024,768]{1,0:T(8,128)(2,1)} %param.29) | copy-start | bytes 4718596
  176.2 18.1 %slice-start.23 = ((s8[4718592]{0:T(1024)(128)(4,1)}), s8[524288]{0:T(1024)(128)(4,1)S(1)}, s32[]{:S(2)}) async-start(s8[4718592]{0:T(1024)(128)(4,1)} %bitcast.429), calls=%async_computation.35 | async-start | bytes 1048576
  178.9 22.1 %copy-start.49 = (f32[512,3072]{1,0:T(8,128)}, f32[512,3072]{1,0:T(8,128)S(1)}, u32[]{:S(2)}) copy-start(f32[512,3072]{1,0:T(8,128)S(1)} %fusion.105) | copy-start | bytes 18874372
  205.2 40.2 %copy-start.23 = (f32[512,768]{1,0:T(8,128)}, f32[512,768]{1,0:T(8,128)S(1)}, u32[]{:S(2)}) copy-start(f32[512,768]{1,0:T(8,128)S(1)} %multiply_add_fusion.2) | copy-start | bytes 4718596
  245.5 20.4 %slice-start.24 = ((s8[4718592]{0:T(1024)(128)(4,1)}), s8[4194304]{0:T(1024)(128)(4,1)S(1)}, s32[]{:S(2)}) async-start(s8[4718592]{0:T(1024)(128)(4,1)} %bitcast.431), calls=%async_computation.36 | async-start | bytes 8388608
  247.1 18.8 %collective-permute-start.3 = (bf16[512,768]{1,0:T(8,128)(2,1)S(1)}, bf16[512,768]{1,0:T(8,128)(2,1)S(1)}, u32[]{:S(2)}, u32[]{:S(2)}) collective-permute-start(bf16[512,768]{1,0:T(8,128)(2,1)S(1)} %get-tuple-element.161), channel_id=1, source_target_pairs={{16,0},{17,1},{18,2},{19,3},{20,4},{21,5},{22,6},{23,7},{24,8},{25... | collective-permute-start | bytes 2359304 | tf_op jit(solution)/shard_map/ppermute | solution.py:16
  249.6 25.7 %copy-start.13 = (f32[512,768]{1,0:T(8,128)}, f32[512,768]{1,0:T(8,128)S(1)}, u32[]{:S(2)}) copy-start(f32[512,768]{1,0:T(8,128)S(1)} %get-tuple-element.193) | copy-start | bytes 4718596
  249.6 16.3 %copy-start.46 = (bf16[1024,768]{1,0:T(8,128)(2,1)S(1)}, bf16[1024,768]{1,0:T(8,128)(2,1)}, u32[]{:S(2)}) copy-start(bf16[1024,768]{1,0:T(8,128)(2,1)} %param.29) | copy-start | bytes 4718596
  249.7 16.3 %slice-start.25 = ((s8[4718592]{0:T(1024)(128)(4,1)}), s8[524288]{0:T(1024)(128)(4,1)S(1)}, s32[]{:S(2)}) async-start(s8[4718592]{0:T(1024)(128)(4,1)} %bitcast.431), calls=%async_computation.37 | async-start | bytes 1048576
  252.4 19.5 %copy-start.10 = (f32[512,3072]{1,0:T(8,128)}, f32[512,3072]{1,0:T(8,128)S(1)}, u32[]{:S(2)}) copy-start(f32[512,3072]{1,0:T(8,128)S(1)} %fusion.101) | copy-start | bytes 18874372
  275.8 87.9 %copy-start.19 = (f32[512,768]{1,0:T(8,128)}, f32[512,768]{1,0:T(8,128)S(1)}, u32[]{:S(2)}) copy-start(f32[512,768]{1,0:T(8,128)S(1)} %multiply_add_fusion) | copy-start | bytes 4718596
  312.1 238.4 %reduce-scatter.9.cloned.1.call-start = ((), (), s32[]{:S(2)}) async-start(), calls=%async_computation.6 | async-start | bytes 17825792 | tf_op jit(solution)/shard_map/reduce_scatter | solution.py:214
  360.2 257.1 %reduce-scatter.13.cloned.1.call-start = ((), (), s32[]{:S(2)}) async-start(), calls=%async_computation.8 | async-start | bytes 2506752 | tf_op jit(solution)/shard_map/reduce_scatter | solution.py:216
  366.4 317.0 %reduce-scatter.11.cloned.1.call-start = ((), (), s32[]{:S(2)}) async-start(), calls=%async_computation.7 | async-start | bytes 2506752 | tf_op jit(solution)/shard_map/reduce_scatter | solution.py:215
  373.4 425.6 %reduce-scatter.15.cloned.1.call-start = ((), (), s32[]{:S(2)}) async-start(), calls=%async_computation.9 | async-start | bytes 10027008 | tf_op jit(solution)/shard_map/reduce_scatter | solution.py:217
  400.6 514.0 %reduce-scatter.17.cloned.1.call-start = ((), (), s32[]{:S(2)}) async-start(), calls=%async_computation.10 | async-start | bytes 10027008 | tf_op jit(solution)/shard_map/reduce_scatter | solution.py:218
  400.9 15.8 %slice-start.2 = ((s8[6291456]{0:T(1024)(128)(4,1)}), s8[4194304]{0:T(1024)(128)(4,1)S(1)}, s32[]{:S(2)}) async-start(s8[6291456]{0:T(1024)(128)(4,1)} %bitcast.371), calls=%async_computation.14 | async-start | bytes 8388608
  (102 other events, 529.3 us)
Sparse Core Ops, SparseCore 0:
  312.2 55.9 reduce-scatter.18
  372.9 177.5 reduce-scatter.8
  555.3 61.8 reduce-scatter.12
  621.4 61.9 reduce-scatter.10
  688.5 110.3 reduce-scatter.14
  803.5 111.1 reduce-scatter.16
where the time goes:
time: 932 us; the launch traced here: 922 us
  waiting for transfers between devices  510 us (55%)
  matrix products  263 us (28%)
  local copies, waits for them, and re-layouts  73.3 us (8%)
  other arithmetic  45.3 us (5%)
  between operations  16 us (2%)
  starting transfers between devices  14.3 us (2%)
    reduce_scatter x1, waiting for transfers between devices, shards(): lax.psum_scatter(totals[5], 'dp', scatter_dimension=1, tiled=True)  116 us
    reduce_scatter x1, waiting for transfers between devices, shards(): lax.psum_scatter(totals[4], 'dp', scatter_dimension=1, tiled=True)  115 us
    reduce_scatter x1, waiting for transfers between devices, shards(): lax.psum_scatter(totals[1], 'dp', scatter_dimension=1, tiled=True)  92.2 us
    reduce_scatter x1, waiting for transfers between devices, shards(): lax.psum_scatter(totals[2], 'dp', scatter_dimension=1, tiled=True)  66.2 us
    reduce_scatter x1, waiting for transfers between devices, shards(): lax.psum_scatter(totals[3], 'dp', scatter_dimension=1, tiled=True)  64.2 us
    sub x3, matrix products, layer_backward(): grad_prob - jnp.sum(grad_prob * prob_full, axis=-1, keepdims=True)  55.7 us
    ppermute x4, waiting for transfers between devices, from_behind(): return lax.ppermute(shard, axis, pairs)  55.6 us
    unnamed x252, local copies, waits for them, and re-layouts  29.2 us
  transfers between devices with their start and end apart: 10, of which 9 were waited for; matrix products, arithmetic and copies ran while one was open for 17% of the time, Pallas kernels for 0%

commit v1 on v0

v1 whole, which is shorter than its diff:
```python
import jax
import jax.numpy as jnp
from jax import lax
from jax.sharding import PartitionSpec as P

L = 512
HD = 64
eps_norm = 1e-06
bf16 = jnp.bfloat16
f32 = jnp.float32
K0 = 0.7978845608028654
K1 = 0.044715


def dot(a, b, ca, cb):
    return lax.dot_general(a, b, (((ca,), (cb,)), ((), ())), preferred_element_type=f32)


def rms_scale(values):
    return lax.rsqrt(jnp.mean(values * values, axis=-1, keepdims=True) + eps_norm)


def gelu_parts(u):
    t = jnp.tanh(K0 * (u + K1 * u * u * u))
    z = 0.5 * u * (1.0 + t)
    g = 0.5 * (1.0 + t) + 0.5 * u * (1.0 - t * t) * (K0 * (1.0 + 3.0 * K1 * u * u))
    return z, g


def forward_row(x, mask, expo, weights):
    gains, w_value, w_out, w_up, w_down = weights
    heads = expo.shape[0]
    length, width = x.shape
    xf = x.astype(f32)
    s1 = rms_scale(xf)
    a1 = (xf * s1 * gains[0]).astype(bf16)
    v = dot(a1, w_value, 1, 0).astype(bf16)
    em = expo * mask[None]
    inv = 1.0 / jnp.sum(em.astype(f32), axis=-1)
    vh = v.reshape(length, heads, HD)
    o = jnp.einsum("hij,jhd->ihd", em, vh, preferred_element_type=f32) * inv.T[:, :, None]
    o = o.astype(bf16).reshape(length, width)
    m = xf + dot(o, w_out, 1, 0)
    s2 = rms_scale(m)
    a2 = (m * s2 * gains[1]).astype(bf16)
    u = dot(a2, w_up, 1, 0)
    z, g = gelu_parts(u)
    z = z.astype(bf16)
    y = (m + dot(z, w_down, 1, 0)).astype(bf16)
    return y, (x, a1, v, inv, o, m, a2, z, g.astype(bf16))


def norm_back(grad, values, gain):
    s = rms_scale(values)
    hat = values * s
    scaled = grad * gain
    back = s * (scaled - hat * jnp.mean(scaled * hat, axis=-1, keepdims=True))
    return back, jnp.sum(grad * hat, axis=0)


def backward_row(dy, res, mask, expo, weights):
    gains, w_value, w_out, w_up, w_down = weights
    x, a1, v, inv, o, m, a2, z, g = res
    heads = expo.shape[0]
    length, width = x.shape
    dz = dot(dy, w_down, 1, 1)
    du = (dz * g.astype(f32)).astype(bf16)
    da2 = dot(du, w_up, 1, 1)
    back2, dg2 = norm_back(da2, m, gains[1])
    dm = dy.astype(f32) + back2
    dml = dm.astype(bf16)
    do = dot(dml, w_out, 1, 1).reshape(length, heads, HD)
    don = (do * inv.T[:, :, None]).astype(bf16)
    em = expo * mask[None]
    dv = jnp.einsum("hij,ihd->jhd", em, don, preferred_element_type=f32)
    dv = dv.reshape(length, width).astype(bf16)
    da1 = dot(dv, w_value, 1, 1)
    back1, dg1 = norm_back(da1, x.astype(f32), gains[0])
    dx = dm + back1
    return dx, (du, dml, don, dv, jnp.stack([dg1, dg2]))


def mixing_row(don, o, v, mask, expo):
    heads = expo.shape[0]
    length = don.shape[0]
    oh = o.reshape(length, heads, HD)
    vh = v.reshape(length, heads, HD)
    delta = jnp.sum(don.astype(f32) * oh.astype(f32), axis=-1).T
    dp = jnp.einsum("ihd,jhd->hij", don, vh, preferred_element_type=f32)
    return (expo * mask[None]).astype(f32) * (dp - delta[:, :, None])


def ring_groups(size):
    zs = size // 4
    return [
        [(z * 2) * 2 + c for z in range(zs)] + [((zs - 1 - z) * 2 + 1) * 2 + c for z in range(zs)]
        for c in range(2)
    ]


def scatter_sum(grad, size):
    rest = grad.shape[1:]
    core = lax.axis_index("dp") % 2
    zs = size // 4
    by = grad.reshape((zs, 2, 2) + rest)
    ring = jnp.concatenate([by[:, 0], by[::-1, 1]], axis=0)
    keep = lax.dynamic_index_in_dim(ring, core, 1, False)
    send = lax.dynamic_index_in_dim(ring, 1 - core, 1, False)
    got = lax.ppermute(send, "dp", [(d, d ^ 1) for d in range(size)])
    total = keep + got
    out = lax.psum_scatter(
        total, "dp", scatter_dimension=0, tiled=True, axis_index_groups=ring_groups(size)
    )
    return out.reshape(rest)


def shards(tokens, segment_ids, cotangent, norm_gains, mixing, w_value, w_out, w_up, w_down):
    size = lax.axis_size("dp")
    is_enc = lax.axis_index("section") == 0
    rows = tokens.shape[0] // L
    weights = (norm_gains[0], w_value[0], w_out[0], w_up[0], w_down[0])
    expo = jnp.exp(mixing[0].astype(f32)).astype(bf16)
    seg = segment_ids.reshape(rows, L)
    pos = lax.broadcasted_iota(jnp.int32, (L, L), 0)
    key = lax.broadcasted_iota(jnp.int32, (L, L), 1)
    masks = [
        ((seg[r][:, None] == seg[r][None, :]) & ((key <= pos) | is_enc)).astype(bf16)
        for r in range(rows)
    ]
    tok = [tokens[r * L : (r + 1) * L] for r in range(rows)]
    cot = [cotangent[r * L : (r + 1) * L] for r in range(rows)]
    sent = []
    for r in range(rows):
        y, _ = forward_row(tok[r], masks[r], expo, weights)
        sent.append(lax.ppermute(y, "section", [(0, 1)]))
    ys, saved, back = [], [], []
    for r in range(rows):
        x = jnp.where(is_enc, tok[r], sent[r])
        y, res = forward_row(x, masks[r], expo, weights)
        ys.append(y)
        saved.append(res)
        dx, _ = backward_row(cot[r], res, masks[r], expo, weights)
        back.append(lax.ppermute(dx.astype(bf16), "section", [(1, 0)]))
    dxs, grads, dys = [], [], []
    mix = 0.0
    gains = 0.0
    for r in range(rows):
        dy = jnp.where(is_enc, back[r], cot[r])
        dx, got = backward_row(dy, saved[r], masks[r], expo, weights)
        dys.append(dy)
        dxs.append(dx)
        grads.append(got)
        mix = mix + mixing_row(got[2], saved[r][4], saved[r][2], masks[r], expo)
        gains = gains + got[4]

    def cat(pieces):
        return jnp.concatenate(pieces, axis=0)

    z = cat([s[7] for s in saved])
    a2 = cat([s[6] for s in saved])
    o = cat([s[4] for s in saved])
    a1 = cat([s[1] for s in saved])
    heads = expo.shape[0]
    width = tokens.shape[1]
    down_t = dot(cat(dys), z, 0, 0).astype(bf16).reshape(size, -1, z.shape[1])
    up_t = dot(cat([g[0] for g in grads]), a2, 0, 0).astype(bf16).reshape(size, -1, width)
    out_t = dot(cat([g[1] for g in grads]), o, 0, 0).astype(bf16).reshape(size, -1, width)
    value_t = dot(cat([g[3] for g in grads]), a1, 0, 0).astype(bf16).reshape(size, -1, width)
    mix_t = mix.astype(bf16).reshape(heads, size, L // size, L).transpose(1, 0, 2, 3)
    gain_t = gains.astype(bf16).reshape(2, size, -1).transpose(1, 0, 2).reshape(size, 1, -1)
    gain_t = jnp.pad(gain_t, ((0, 0), (0, 15), (0, width - gain_t.shape[2])))
    per = width // size
    down_g = scatter_sum(down_t, size).astype(f32).T
    up_g = scatter_sum(up_t, size).astype(f32).T
    mix_g = scatter_sum(mix_t, size).astype(f32)
    small = scatter_sum(jnp.concatenate([out_t, value_t, gain_t], axis=1), size).astype(f32)
    out_g = small[:per].T
    value_g = small[per : 2 * per].T
    gains_g = small[2 * per, : 2 * per].reshape(2, per)
    return (
        cat(ys)[None],
        cat(dxs)[None],
        gains_g[None],
        mix_g[None],
        value_g[None],
        out_g[None],
        up_g[None],
        down_g[None],
    )


def solution(mesh):
    placed = (
        P("dp", None),
        P("dp"),
        P("dp", None),
        P("section", None, None),
        P("section", None, None, None),
        P("section", None, None),
        P("section", None, None),
        P("section", None, None),
        P("section", None, None),
    )
    return jax.shard_map(
        shards,
        mesh=mesh,
        in_specs=placed,
        out_specs=(
            P("section", "dp", None),
            P("section", "dp", None),
            P("section", None, "dp"),
            P("section", None, "dp", None),
            P("section", None, "dp"),
            P("section", None, "dp"),
            P("section", None, "dp"),
            P("section", None, "dp"),
        ),
        check_vma=False,
    )
```

time: 932 us -> 449 us (0.48)
  waiting for transfers between devices: 510 us -> 132 us
  matrix products: 263 us -> 203 us
  local copies, waits for them, and re-layouts: 73.3 us -> 34.7 us
    reduce_scatter x5 -> x4, waiting for transfers between devices: 454 us -> 73.3 us  [scatter_sum(): lax.psum_scatter(total, 'dp', scatter_dimension=0, tiled=True, axis_index...]
    sub x3 -> x0, matrix products: 55.7 us -> none  [layer_backward(): grad_prob - jnp.sum(grad_prob * prob_full, axis=-1, keepdims=True)]
    unnamed x252 -> x180, local copies, waits for them, and re-layouts: 29.2 us -> 10.5 us
    add x1 -> x0, local copies, waits for them, and re-layouts: 18.4 us -> none  [add_grads(): return tuple((left + right for left, right in zip(totals, extra)))]
    another operation x5 -> x0, other arithmetic: 13.2 us -> none
    convert_element_type x9 -> x4, local copies, waits for them, and re-layouts: 17.6 us -> 6.27 us  [forward_row(): v = dot(a1, w_value, 1, 0).astype(bf16)]
    dot_general x56 -> x42, matrix products: 208 us -> 203 us  [the longest x32 147 us: dot(): lax.dot_general(a, b, (((ca,), (cb,)), ((), ())), preferred_element_type=...]
    ppermute x4 -> x8, waiting for transfers between devices: 55.6 us -> 58.3 us  [the longest x2 36.1 us: shards(): back.append(lax.ppermute(dx.astype(bf16), 'section', [(1, 0)]))]
  transfers between devices with their start and end apart: 10 -> 12, of which waited for: 9 -> 7; matrix products, arithmetic and copies ran while one was open for 17% -> 20% of each run, Pallas kernels for 0% -> 0%
where the time goes in v1:
time: 449 us; the launch traced here: 440 us
  matrix products  203 us (45%)
  waiting for transfers between devices  132 us (29%)
  other arithmetic  44.9 us (10%)
  local copies, waits for them, and re-layouts  34.7 us (8%)
  between operations  15.3 us (3%)
  starting transfers between devices  10.7 us (2%)
    dot_general x32, matrix products, dot(): lax.dot_general(a, b, (((ca,), (cb,)), ((), ())), preferred_element_type=...  147 us
    reduce_scatter x4, waiting for transfers between devices, scatter_sum(): lax.psum_scatter(total, 'dp', scatter_dimension=0, tiled=True, axis_index...  73.3 us
    ppermute x2, waiting for transfers between devices, shards(): back.append(lax.ppermute(dx.astype(bf16), 'section', [(1, 0)]))  36.1 us
    dot_general x4, matrix products, backward_row(): dv = jnp.einsum('hij,ihd->jhd', em, don, preferred_element_type=f32)  20 us
    dot_general x4, matrix products, forward_row(): jnp.einsum('hij,jhd->ihd', em, vh, preferred_element_type=f32)  19.9 us
    ppermute x2, waiting for transfers between devices, shards(): sent.append(lax.ppermute(y, 'section', [(0, 1)]))  16.5 us
    dot_general x2, matrix products, mixing_row(): dp = jnp.einsum('ihd,jhd->hij', don, vh, preferred_element_type=f32)  16.5 us
    unnamed x180, local copies, waits for them, and re-layouts  10.5 us
  transfers between devices with their start and end apart: 12, of which 7 were waited for; matrix products, arithmetic and copies ran while one was open for 20% of the time, Pallas kernels for 0%

profile of v1, /device:TPU:0, one launch (start us, length us, event | category | flops | bytes accessed | tf_op | source)
XLA Modules:
  0.0 440.2 jit_solution(16107215502390248913)
XLA Ops:
  14.6 6.5 %convert_reduce_fusion.1 = (f32[12,512]{1,0:T(8,128)S(1)}, f32[12,512]{1,0:T(8,128)S(1)}) fusion(bf16[512,512]{1,0:T(8,128)(2,1)S(1)} %get-tuple-element.81, bf16[1,12,512,512]{3,2,1,0:T(8,128)(2,1)} %param.13, bf16[512,512]{1,0:T(8,128)(2,1)S(1)} %get-tuple-element.82), kind=kLoop, calls=%fused_computation.3 | loop fusion | flops 25153536 | bytes 7389184 | tf_op jit(solution)/shard_map/reduce_sum | solution.py:39
  24.8 4.4 fusion.10
  29.2 3.5 add_convert_fusion.3
  32.7 5.9 %collective-permute-start = (bf16[512,768]{1,0:T(8,128)(2,1)}, bf16[512,768]{1,0:T(8,128)(2,1)}, u32[]{:S(2)}, u32[]{:S(2)}) collective-permute-start(bf16[512,768]{1,0:T(8,128)(2,1)} %add_convert_fusion.3), channel_id=1, source_target_pairs={{0,16},{1,17},{2,18},{3,19},{4,20},{5,21},{6,22},{7,23},{8,24},{9,... | collective-permute-start | bytes 2359304 | tf_op jit(solution)/shard_map/ppermute | solution.py:135
  42.7 5.4 %fusion.157 = bf16[512,12,64]{0,2,1:T(8,128)(2,1)S(1)} fusion(bf16[512,12,64]{0,2,1:T(8,128)(2,1)} %bitcast.339, f32[512,12]{0,1:T(8,128)S(1)} %divide_bitcast_fusion, bf16[1,12,512,512]{3,2,1,0:T(8,128)(2,1)} %param.13, bf16[512,512]{1,0:T(8,128)(2,1)S(1)} %get-tuple-element.82), kind=kOutput, calls=%fused_computation.205 | convolution fusion | flops 412876800 | bytes 8413184 | tf_op jit(solution)/shard_map/hij,jhd->ihd/dot_general | solution.py:41
  49.0 6.9 %fusion.17 = bf16[512,3072]{1,0:T(8,128)(2,1)S(1)} fusion(bf16[1,768,3072]{2,1,0:T(8,128)(2,1)} %param.16, f32[512,768]{1,0:T(8,128)S(1)} %get-tuple-element.54, f32[512]{0:T(512)S(1)} %add_rsqrt_fusion.2, f32[768]{0:T(1024)S(1)} %get-tuple-element.20), kind=kOutput, calls=%fused_computation.36 | convolution fusion | flops 2431254528 | bytes 9442304 | tf_op jit(solution)/shard_map/dot_general | solution.py:16
  60.1 16.5 %collective-permute-done.1 = bf16[512,768]{1,0:T(8,128)(2,1)S(1)} collective-permute-done((bf16[512,768]{1,0:T(8,128)(2,1)S(1)}, bf16[512,768]{1,0:T(8,128)(2,1)S(1)}, u32[]{:S(2)}, u32[]{:S(2)}) %collective-permute-start.1) | collective-permute-done | bytes 786464 | tf_op jit(solution)/shard_map/ppermute | solution.py:135
  82.7 6.5 %fusion.158 = bf16[512,12,64]{0,2,1:T(8,128)(2,1)} fusion(bf16[512,12,64]{0,2,1:T(8,128)(2,1)S(1)} %bitcast.331, f32[512,12]{0,1:T(8,128)} %copy-done.45, bf16[1,12,512,512]{3,2,1,0:T(8,128)(2,1)} %param.13, bf16[512,512]{1,0:T(8,128)(2,1)} %copy-done.23), kind=kOutput, calls=%fused_computation.207 | convolution fusion | flops 412876800 | bytes 8413184 | tf_op jit(solution)/shard_map/hij,jhd->ihd/dot_general | solution.py:41
  92.3 5.4 %fusion.156 = bf16[512,12,64]{0,2,1:T(8,128)(2,1)S(1)} fusion(bf16[512,12,64]{0,2,1:T(8,128)(2,1)S(1)} %bitcast.336, f32[512,12]{0,1:T(8,128)S(1)} %copy-done.43, bf16[1,12,512,512]{3,2,1,0:T(8,128)(2,1)} %param.13, bf16[512,512]{1,0:T(8,128)(2,1)S(1)} %copy-done.26), kind=kOutput, calls=%fused_computation.203 | convolution fusion | flops 412876800 | bytes 8413184 | tf_op jit(solution)/shard_map/hij,jhd->ihd/dot_general | solution.py:41
  101.5 6.6 %multiply_convert_fusion.1 = (bf16[512,3072]{1,0:T(8,128)(2,1)}, f32[512,3072]{1,0:T(8,128)}) fusion(bf16[512,768]{1,0:T(8,128)(2,1)S(1)} %get-tuple-element.45, bf16[1,768,3072]{2,1,0:T(8,128)(2,1)S(1)} %bitcast.343), kind=kOutput, calls=%fused_computation.59 | convolution fusion | flops 2430074880 | bytes 14942208 | tf_op jit(solution)/shard_map/dot_general | solution.py:16
  108.1 14.3 %multiply_reduce_fusion.7 = (f32[512]{0:T(512)}, f32[512,768]{1,0:T(8,128)}) fusion(f32[512,768]{1,0:T(8,128)} %copy-done.3, f32[512]{0:T(512)S(1)} %add_rsqrt_fusion.4, f32[768]{0:T(1024)S(1)} %get-tuple-element.20, bf16[1,768,3072]{2,1,0:T(8,128)(2,1)} %param.16, bf16[1,3072,768]{2,1,0:T(8,128)(2,1)} %param.17, bf16[1024,768]{1,0:T(8,128)(2,1)} %param.11, ...), kind=kOutput, calls=%fused_computation.225 | convolution fusion | flops 4866440704 | bytes 19667968 | tf_op jit(solution)/shard_map/dot_general | solution.py:16
  123.6 7.9 %convolution_convert_fusion.7 = bf16[12,64,512]{2,1,0:T(8,128)(2,1)} fusion(bf16[12,64,768]{2,1,0:T(8,128)(2,1)S(1)} %bitcast.320, f32[512,12]{0,1:T(8,128)} %copy-done.45, f32[512,768]{1,0:T(8,128)} %get-tuple-element.64, f32[512,768]{1,0:T(8,128)} %copy-done.3, f32[512]{0:T(512)} %broadcast_multiply_fusion.7, f32[512]{0:T(512)S(1)} %add_rsqrt_fusion.4, ...), kind=kOutput, calls=%fused_computation.251 | convolution fusion | flops 1020002304 | bytes 12750848 | tf_op jit(solution)/shard_map/hij,ihd->jhd/dot_general | solution.py:75
  131.5 3.9 fusion.110
  136.0 8.6 %multiply_convert_fusion = (bf16[512,3072]{1,0:T(8,128)(2,1)}, f32[512,3072]{1,0:T(8,128)}) fusion(bf16[512,768]{1,0:T(8,128)(2,1)S(1)} %copy-done.32, bf16[1,768,3072]{2,1,0:T(8,128)(2,1)} %param.16), kind=kOutput, calls=%fused_computation.58 | convolution fusion | flops 2430074880 | bytes 14942208 | tf_op jit(solution)/shard_map/dot_general | solution.py:16
  144.6 13.9 %multiply_reduce_fusion.5 = (f32[512]{0:T(512)}, f32[512,768]{1,0:T(8,128)}) fusion(f32[512,768]{1,0:T(8,128)S(1)} %get-tuple-element.58, f32[512]{0:T(512)S(1)} %add_rsqrt_fusion, f32[768]{0:T(1024)S(1)} %get-tuple-element.20, bf16[1,768,3072]{2,1,0:T(8,128)(2,1)} %param.16, bf16[1,3072,768]{2,1,0:T(8,128)(2,1)} %param.17, bf16[1024,768]{1,0:T(8,128)(2,1)} %param.11, ...), kind=kOutput, calls=%fused_computation.219 | convolution fusion | flops 4866440704 | bytes 19667968 | tf_op jit(solution)/shard_map/dot_general | solution.py:16
  159.7 7.5 %convolution_convert_fusion.5 = bf16[12,64,512]{2,1,0:T(8,128)(2,1)} fusion(bf16[12,64,768]{2,1,0:T(8,128)(2,1)S(1)} %bitcast.322, f32[512,12]{0,1:T(8,128)} %copy-done.42, f32[512,768]{1,0:T(8,128)} %get-tuple-element.68, f32[512,768]{1,0:T(8,128)S(1)} %get-tuple-element.58, f32[512]{0:T(512)} %broadcast_multiply_fusion.3, f32[512]{0:T(512)S(1)} %add_rsqrt_fusion, ...), kind=kOutput, calls=%fused_computation.249 | convolution fusion | flops 1020002304 | bytes 12750848 | tf_op jit(solution)/shard_map/hij,ihd->jhd/dot_general | solution.py:75
  170.0 4.0 fusion.114
  176.7 21.0 %collective-permute-done.2 = bf16[512,768]{1,0:T(8,128)(2,1)} collective-permute-done((bf16[512,768]{1,0:T(8,128)(2,1)}, bf16[512,768]{1,0:T(8,128)(2,1)}, u32[]{:S(2)}, u32[]{:S(2)}) %collective-permute-start.2) | collective-permute-done | bytes 786464 | tf_op jit(solution)/shard_map/ppermute | solution.py:143
  197.7 15.1 %collective-permute-done.3 = bf16[512,768]{1,0:T(8,128)(2,1)} collective-permute-done((bf16[512,768]{1,0:T(8,128)(2,1)}, bf16[512,768]{1,0:T(8,128)(2,1)}, u32[]{:S(2)}, u32[]{:S(2)}) %collective-permute-start.3) | collective-permute-done | bytes 786464 | tf_op jit(solution)/shard_map/ppermute | solution.py:143
  215.0 9.9 %fusion.5 = bf16[512,3072]{1,0:T(8,128)(2,1)} fusion(bf16[512,768]{1,0:T(8,128)(2,1)S(1)} %get-tuple-element.35, bf16[1,3072,768]{2,1,0:T(8,128)(2,1)} %param.17, f32[512,3072]{1,0:T(8,128)} %get-tuple-element.60), kind=kOutput, calls=%fused_computation.24 | convolution fusion | flops 2448949248 | bytes 14942208 | tf_op jit(solution)/shard_map/dot_general | solution.py:16
  224.9 7.7 %fusion.3 = bf16[512,3072]{1,0:T(8,128)(2,1)S(1)} fusion(bf16[512,768]{1,0:T(8,128)(2,1)S(1)} %get-tuple-element.34, bf16[1,3072,768]{2,1,0:T(8,128)(2,1)} %param.17, f32[512,3072]{1,0:T(8,128)S(1)} %bitcast.365), kind=kOutput, calls=%fused_computation.22 | convolution fusion | flops 2448949248 | bytes 14942208 | tf_op jit(solution)/shard_map/dot_general | solution.py:16
  232.6 3.3 multiply_reduce_fusion.3
  243.8 7.5 %multiply_reduce_fusion.2 = (f32[768]{0:T(1024)}, f32[512]{0:T(512)S(1)}, f32[512,768]{1,0:T(8,128)}, f32[512,768]{1,0:T(8,128)S(1)}) fusion(f32[512,768]{1,0:T(8,128)S(1)} %get-tuple-element.58, f32[512]{0:T(512)S(1)} %add_rsqrt_fusion, f32[768]{0:T(1024)S(1)} %get-tuple-element.20, f32[512]{0:T(512)S(1)} %broadcast_multiply_fusion.4, ...), kind=kOutput, calls=%fused_computation.212 | convolution fusion | flops 2423782144 | bytes 18895872 | tf_op jit(solution)/shard_map/dot_general | solution.py:16
  278.7 5.6 %fusion.44 = bf16[3072,768]{1,0:T(8,128)(2,1)S(1)} fusion(bf16[512,3072]{1,0:T(8,128)(2,1)S(1)} %copy-done.70, bf16[512,3072]{1,0:T(8,128)(2,1)S(1)} %copy-done.72, bf16[512,768]{1,0:T(8,128)(2,1)S(1)} %copy-done.33, bf16[512,768]{1,0:T(8,128)(2,1)S(1)} %copy-done.31), kind=kOutput, calls=%fused_computation.71 | convolution fusion | flops 4849926144 | bytes 12582912 | tf_op jit(solution)/shard_map/dot_general | solution.py:16
  292.1 8.9 %fusion.41 = bf16[768,3072]{1,0:T(8,128)(2,1)} fusion(bf16[512,3072]{1,0:T(8,128)(2,1)} %get-tuple-element.59, bf16[512,3072]{1,0:T(8,128)(2,1)S(1)} %copy-done.73, bf16[512,768]{1,0:T(8,128)(2,1)S(1)} %copy-done.7, bf16[512,768]{1,0:T(8,128)(2,1)S(1)} %copy-done.20), kind=kOutput, calls=%fused_computation.70 | convolution fusion | flops 4849926144 | bytes 12582912 | tf_op jit(solution)/shard_map/dot_general | solution.py:16
  307.4 6.4 %fusion.272 = f32[12,512,512]{2,1,0:T(8,128)} fusion(bf16[512,12,64]{0,2,1:T(8,128)(2,1)S(1)} %copy-done.35, bf16[512,12,64]{0,2,1:T(8,128)(2,1)S(1)} %bitcast.332), kind=kOutput, calls=%fused_computation.344 | convolution fusion | flops 402653184 | bytes 14155776 | tf_op jit(solution)/shard_map/ihd,jhd->hij/dot_general | solution.py:89
  315.5 10.1 %fusion.1 = bf16[12,512,512]{2,1,0:T(8,128)(2,1)S(1)} fusion(f32[12,512,512]{2,1,0:T(8,128)} %fusion.272, f32[12,512]{1,0:T(8,128)} %bitcast.363, f32[12,512]{1,0:T(8,128)} %bitcast.362, bf16[512,12,64]{0,2,1:T(8,128)(2,1)} %copy-done.69, bf16[512,12,64]{0,2,1:T(8,128)(2,1)} %bitcast.337, bf16[512,512]{1,0:T(8,128)(2,1)} %copy-done.23, ...), kind=kOutput, calls=%fused_computation.5 | convolution fusion | flops 440401920 | bytes 27836416 | tf_op jit(solution)/shard_map/ihd,jhd->hij/dot_general | solution.py:89
  327.3 5.6 %collective-permute-done.5 = bf16[8,12,32,512]{3,2,1,0:T(8,128)(2,1)S(1)} collective-permute-done((bf16[8,12,32,512]{3,2,1,0:T(8,128)(2,1)S(1)}, bf16[8,12,32,512]{3,2,1,0:T(8,128)(2,1)S(1)}, u32[]{:S(2)}, u32[]{:S(2)}) %collective-permute-start.5) | collective-permute-done | bytes 3145760 | tf_op jit(solution)/shard_map/ppermute | solution.py:109
  334.9 6.6 %add_convert_fusion.2 = bf16[512,768]{1,0:T(8,128)(2,1)S(1)} fusion(f32[512,768]{1,0:T(8,128)} %copy-done.3, bf16[512,3072]{1,0:T(8,128)(2,1)} %get-tuple-element.61, bf16[1,3072,768]{2,1,0:T(8,128)(2,1)} %param.17), kind=kOutput, calls=%fused_computation.232 | convolution fusion | flops 2416705536 | bytes 10223616 | tf_op jit(solution)/shard_map/dot_general | solution.py:16
  341.5 5.1 %add_convert_fusion = bf16[512,768]{1,0:T(8,128)(2,1)S(1)} fusion(f32[512,768]{1,0:T(8,128)S(1)} %get-tuple-element.58, bf16[512,3072]{1,0:T(8,128)(2,1)S(1)} %copy-done.74, bf16[1,3072,768]{2,1,0:T(8,128)(2,1)} %param.17), kind=kOutput, calls=%fused_computation.226 | convolution fusion | flops 2416705536 | bytes 10223616 | tf_op jit(solution)/shard_map/dot_general | solution.py:16
  357.3 34.1 %reduce-scatter.11.cloned.1.call-done = bf16[1,48,3072]{2,1,0:T(8,128)(2,1)} async-done(((bf16[8,48,3072]{2,1,0:T(8,128)(2,1)}), bf16[1,48,3072]{2,1,0:T(8,128)(2,1)}) %reduce-scatter.11.cloned.1.call-update) | async-done | bytes 294928 | tf_op jit(solution)/shard_map/reduce_scatter | solution.py:111
  393.1 38.3 %reduce-scatter.7.cloned.1.call-done = bf16[1,12,32,512]{3,2,1,0:T(8,128)(2,1)} async-done(((bf16[8,12,32,512]{3,2,1,0:T(8,128)(2,1)}), bf16[1,12,32,512]{3,2,1,0:T(8,128)(2,1)}) %reduce-scatter.7.cloned.1.call-update) | async-done | bytes 393232 | tf_op jit(solution)/shard_map/reduce_scatter | solution.py:111
  (292 shorter events, 112.0 us)
Async XLA Ops:
  7.2 16.6 %copy-start = (bf16[1,768,768]{2,1,0:T(8,128)(2,1)S(1)}, bf16[1,768,768]{2,1,0:T(8,128)(2,1)}, u32[]{:S(2)}) copy-start(bf16[1,768,768]{2,1,0:T(8,128)(2,1)} %param.15) | copy-start | bytes 3538948
  7.2 345.0 %reduce-scatter.5.cloned.1.call-start = ((), (), s32[]{:S(2)}) async-start(), calls=%async_computation.4 | async-start | bytes 1548288 | tf_op jit(solution)/shard_map/reduce_scatter | solution.py:111
  14.5 6.6 %copy-start.23 = (bf16[512,512]{1,0:T(8,128)(2,1)}, bf16[512,512]{1,0:T(8,128)(2,1)S(1)}, u32[]{:S(2)}) copy-start(bf16[512,512]{1,0:T(8,128)(2,1)S(1)} %get-tuple-element.81) | copy-start | bytes 1572868
  14.5 28.1 %copy-start.25 = (bf16[512,512]{1,0:T(8,128)(2,1)}, bf16[512,512]{1,0:T(8,128)(2,1)S(1)}, u32[]{:S(2)}) copy-start(bf16[512,512]{1,0:T(8,128)(2,1)S(1)} %get-tuple-element.82) | copy-start | bytes 1572868
  14.5 6.6 %copy-start.13 = (bf16[1,12,512,512]{3,2,1,0:T(8,128)(2,1)S(1)}, bf16[1,12,512,512]{3,2,1,0:T(8,128)(2,1)}, u32[]{:S(2)}) copy-start(bf16[1,12,512,512]{3,2,1,0:T(8,128)(2,1)} %param.13) | copy-start | bytes 18874372
  14.6 10.2 %slice-start.2 = ((s8[4718592]{0:T(1024)(128)(4,1)}), s8[4194304]{0:T(1024)(128)(4,1)S(1)}, s32[]{:S(2)}) async-start(s8[4718592]{0:T(1024)(128)(4,1)} %bitcast.340), calls=%async_computation.10 | async-start | bytes 8388608
  29.2 9.4 %copy-start.59 = (bf16[1,768,768]{2,1,0:T(8,128)(2,1)S(1)}, bf16[1,768,768]{2,1,0:T(8,128)(2,1)}, u32[]{:S(2)}) copy-start(bf16[1,768,768]{2,1,0:T(8,128)(2,1)} %param.14) | copy-start | bytes 3538948
  32.7 27.5 %collective-permute-start = (bf16[512,768]{1,0:T(8,128)(2,1)}, bf16[512,768]{1,0:T(8,128)(2,1)}, u32[]{:S(2)}, u32[]{:S(2)}) collective-permute-start(bf16[512,768]{1,0:T(8,128)(2,1)} %add_convert_fusion.3), channel_id=1, source_target_pairs={{0,16},{1,17},{2,18},{3,19},{4,20},{5,21},{6,22},{7,23},{8,24},{9,... | collective-permute-start | bytes 2359304 | tf_op jit(solution)/shard_map/ppermute | solution.py:135
  48.1 7.9 %slice-start.10 = ((s8[4718592]{0:T(1024)(128)(4,1)}), s8[4194304]{0:T(1024)(128)(4,1)S(1)}, s32[]{:S(2)}) async-start(s8[4718592]{0:T(1024)(128)(4,1)} %bitcast.348), calls=%async_computation.18 | async-start | bytes 8388608
  49.0 6.9 %slice-start.11 = ((s8[4718592]{0:T(1024)(128)(4,1)}), s8[524288]{0:T(1024)(128)(4,1)S(1)}, s32[]{:S(2)}) async-start(s8[4718592]{0:T(1024)(128)(4,1)} %bitcast.348), calls=%async_computation.19 | async-start | bytes 1048576
  55.9 20.7 %copy-start.15 = (bf16[1024,768]{1,0:T(8,128)(2,1)S(1)}, bf16[1024,768]{1,0:T(8,128)(2,1)}, u32[]{:S(2)}) copy-start(bf16[1024,768]{1,0:T(8,128)(2,1)} %param.9) | copy-start | bytes 4718596
  58.6 18.1 %collective-permute-start.1 = (bf16[512,768]{1,0:T(8,128)(2,1)S(1)}, bf16[512,768]{1,0:T(8,128)(2,1)S(1)}, u32[]{:S(2)}, u32[]{:S(2)}) collective-permute-start(bf16[512,768]{1,0:T(8,128)(2,1)S(1)} %add_convert_fusion.1), channel_id=1, source_target_pairs={{0,16},{1,17},{2,18},{3,19},{4,20},{5,21},{6,22},{7,23},{8,24},{9,... | collective-permute-start | bytes 2359304 | tf_op jit(solution)/shard_map/ppermute | solution.py:135
  174.1 23.7 %collective-permute-start.2 = (bf16[512,768]{1,0:T(8,128)(2,1)}, bf16[512,768]{1,0:T(8,128)(2,1)}, u32[]{:S(2)}, u32[]{:S(2)}) collective-permute-start(bf16[512,768]{1,0:T(8,128)(2,1)} %get-tuple-element.36), channel_id=1, source_target_pairs={{16,0},{17,1},{18,2},{19,3},{20,4},{21,5},{22,6},{23,7},{24,8},{25... | collective-permute-start | bytes 2359304 | tf_op jit(solution)/shard_map/ppermute | solution.py:143
  175.3 37.4 %collective-permute-start.3 = (bf16[512,768]{1,0:T(8,128)(2,1)}, bf16[512,768]{1,0:T(8,128)(2,1)}, u32[]{:S(2)}, u32[]{:S(2)}) collective-permute-start(bf16[512,768]{1,0:T(8,128)(2,1)} %get-tuple-element.37), channel_id=1, source_target_pairs={{16,0},{17,1},{18,2},{19,3},{20,4},{21,5},{22,6},{23,7},{24,8},{25... | collective-permute-start | bytes 2359304 | tf_op jit(solution)/shard_map/ppermute | solution.py:143
  212.8 12.1 %slice-start.12 = ((s8[6291456]{0:T(1024)(128)(4,1)}), s8[4194304]{0:T(1024)(128)(4,1)S(1)}, s32[]{:S(2)}) async-start(s8[6291456]{0:T(1024)(128)(4,1)} %bitcast.364), calls=%async_computation.20 | async-start | bytes 8388608
  214.9 28.9 %copy-start.19 = (bf16[512,768]{1,0:T(8,128)(2,1)}, bf16[512,768]{1,0:T(8,128)(2,1)S(1)}, u32[]{:S(2)}) copy-start(bf16[512,768]{1,0:T(8,128)(2,1)S(1)} %get-tuple-element.34) | copy-start | bytes 2359300
  214.9 36.3 %copy-start.6 = (bf16[512,768]{1,0:T(8,128)(2,1)}, bf16[512,768]{1,0:T(8,128)(2,1)S(1)}, u32[]{:S(2)}) copy-start(bf16[512,768]{1,0:T(8,128)(2,1)S(1)} %get-tuple-element.35) | copy-start | bytes 2359300
  214.9 9.9 %slice-start.13 = ((s8[6291456]{0:T(1024)(128)(4,1)}), s8[2097152]{0:T(1024)(128)(4,1)S(1)}, s32[]{:S(2)}) async-start(s8[6291456]{0:T(1024)(128)(4,1)} %bitcast.364), calls=%async_computation.21 | async-start | bytes 4194304
  214.9 17.6 %slice-start.6 = ((s8[4718592]{0:T(1024)(128)(4,1)}), s8[4194304]{0:T(1024)(128)(4,1)S(1)}, s32[]{:S(2)}) async-start(s8[4718592]{0:T(1024)(128)(4,1)} %bitcast.344), calls=%async_computation.14 | async-start | bytes 8388608
  215.0 23.6 %slice-start = ((s8[6291456]{0:T(1024)(128)(4,1)}), s8[4194304]{0:T(1024)(128)(4,1)S(1)}, s32[]{:S(2)}) async-start(s8[6291456]{0:T(1024)(128)(4,1)} %bitcast.326), calls=%async_computation.8 | async-start | bytes 8388608
  224.9 7.7 %slice-start.7 = ((s8[4718592]{0:T(1024)(128)(4,1)}), s8[524288]{0:T(1024)(128)(4,1)S(1)}, s32[]{:S(2)}) async-start(s8[4718592]{0:T(1024)(128)(4,1)} %bitcast.344), calls=%async_computation.15 | async-start | bytes 1048576
  224.9 7.7 %copy-start.5 = (f32[512,768]{1,0:T(8,128)S(1)}, f32[512,768]{1,0:T(8,128)}, u32[]{:S(2)}) copy-start(f32[512,768]{1,0:T(8,128)} %copy-done.3) | copy-start | bytes 4718596
  224.9 13.7 %slice-start.1 = ((s8[6291456]{0:T(1024)(128)(4,1)}), s8[2097152]{0:T(1024)(128)(4,1)S(1)}, s32[]{:S(2)}) async-start(s8[6291456]{0:T(1024)(128)(4,1)} %bitcast.326), calls=%async_computation.9 | async-start | bytes 4194304
  275.9 11.8 %collective-permute-start.4 = (bf16[8,112,768]{2,1,0:T(8,128)(2,1)S(1)}, bf16[8,112,768]{2,1,0:T(8,128)(2,1)S(1)}, u32[]{:S(2)}, u32[]{:S(2)}) collective-permute-start(bf16[8,112,768]{2,1,0:T(8,128)(2,1)S(1)} %fusion.185), channel_id=1, source_target_pairs={{0,1},{1,0},{2,3},{3,2},{4,5},{5,4},{6,7},{7,6},{8,9},{9,8},{10,11... | collective-permute-start | bytes 4128776 | tf_op jit(solution)/shard_map/ppermute | solution.py:109
  289.0 66.5 %reduce-scatter.9.cloned.1.call-start = ((), (), s32[]{:S(2)}) async-start(), calls=%async_computation.6 | async-start | bytes 2654208 | tf_op jit(solution)/shard_map/reduce_scatter | solution.py:111
  291.1 10.0 %collective-permute-start.6 = (bf16[8,192,768]{2,1,0:T(8,128)(2,1)S(1)}, bf16[8,192,768]{2,1,0:T(8,128)(2,1)S(1)}, u32[]{:S(2)}, u32[]{:S(2)}) collective-permute-start(bf16[8,192,768]{2,1,0:T(8,128)(2,1)S(1)} %fusion.102), channel_id=1, source_target_pairs={{0,1},{1,0},{2,3},{3,2},{4,5},{5,4},{6,7},{7,6},{8,9},{9,8},{10,11... | collective-permute-start | bytes 7077896 | tf_op jit(solution)/shard_map/ppermute | solution.py:109
  292.1 8.9 %copy-start.1 = (bf16[4,2,192,768]{3,2,1,0:T(8,128)(2,1)S(1)}, bf16[4,2,192,768]{3,2,1,0:T(8,128)(2,1)}, u32[]{:S(2)}) copy-start(bf16[4,2,192,768]{3,2,1,0:T(8,128)(2,1)} %reverse_bitcast_fusion.2) | copy-start | bytes 7077892
  292.1 8.9 %copy-start.2 = (bf16[4,2,192,768]{3,2,1,0:T(8,128)(2,1)S(1)}, bf16[4,2,192,768]{3,2,1,0:T(8,128)(2,1)}, u32[]{:S(2)}) copy-start(bf16[4,2,192,768]{3,2,1,0:T(8,128)(2,1)} %get-tuple-element.31) | copy-start | bytes 7077892
  302.8 88.5 %reduce-scatter.11.cloned.1.call-start = ((), (), s32[]{:S(2)}) async-start(), calls=%async_computation.7 | async-start | bytes 2654208 | tf_op jit(solution)/shard_map/reduce_scatter | solution.py:111
  306.2 7.6 %collective-permute-start.7 = (bf16[8,48,3072]{2,1,0:T(8,128)(2,1)S(1)}, bf16[8,48,3072]{2,1,0:T(8,128)(2,1)S(1)}, u32[]{:S(2)}, u32[]{:S(2)}) collective-permute-start(bf16[8,48,3072]{2,1,0:T(8,128)(2,1)S(1)} %fusion.97), channel_id=1, source_target_pairs={{0,1},{1,0},{2,3},{3,2},{4,5},{5,4},{6,7},{7,6},{8,9},{9,8},{10,11... | collective-permute-start | bytes 7077896 | tf_op jit(solution)/shard_map/ppermute | solution.py:109
  315.5 116.0 %reduce-scatter.7.cloned.1.call-start = ((), (), s32[]{:S(2)}) async-start(), calls=%async_computation.5 | async-start | bytes 3538944 | tf_op jit(solution)/shard_map/reduce_scatter | solution.py:111
  327.2 5.7 %collective-permute-start.5 = (bf16[8,12,32,512]{3,2,1,0:T(8,128)(2,1)S(1)}, bf16[8,12,32,512]{3,2,1,0:T(8,128)(2,1)S(1)}, u32[]{:S(2)}, u32[]{:S(2)}) collective-permute-start(bf16[8,12,32,512]{3,2,1,0:T(8,128)(2,1)S(1)} %fusion.80), channel_id=1, source_target_pairs={{0,1},{1,0},{2,3},{3,2},{4,5},{5,4},{6,7},{7,6},{8,9},{9,8},{10,11... | collective-permute-start | bytes 9437192 | tf_op jit(solution)/shard_map/ppermute | solution.py:109
  (69 other events, 202.9 us)
Sparse Core Ops, SparseCore 0:
  289.1 30.4 reduce-scatter.4
  322.0 33.3 reduce-scatter.8
  357.9 33.4 reduce-scatter.10
  393.6 37.8 reduce-scatter.6
